TPU v7x, 32 devices: a whole 2x2x4 slice. The times are simulated.
32 devices in a mesh: row: 8 (over z, x), col: 4 (over y, core).
Axes of the slice: x: 2, y: 2, z: 4, core: 2. Of those that a mesh axis runs over, the one named last changes fastest.
Arguments:
- tiles: bfloat16 [8, 4, 64, 128, 128], P('row', 'col'), may hold values from -0.078125 to 0.078125
- positions: int32 [8, 4, 64], replicated, may hold values from 0 to 15, as said below
- demand: bfloat16 [16384, 128], P(('row', 'col')), may hold values from -6 to 6
- value_added: bfloat16 [16384, 128], P(('row', 'col')), may hold values from -6 to 6
- extracted: int32 [128], replicated, may hold values from 0 to 127
Outputs:
- quantity: float32 [16384, 128], P(('row', 'col'))
- price: float32 [16384, 128], P(('row', 'col'))
Inputs may be any that keep to these rules, and one draw needn't show every extreme that they name: Within each device's slots d * 2 to d * 2 + 1 the 2 positions differ.
All inputs are finite; a program needn't handle non-finite values.
Results may differ from a plain program's by a relative error of at most 0.0011.
Values may be sent and summed in bfloat16 or wider, within the bound.
A program may use at most 192 MiB of HBM per device.

v0:
```python
import jax
import jax.numpy as jnp
from jax import lax
from jax.sharding import PartitionSpec as P

TERMS = 3
GROUPS = 128


def supply_term(vector, own_tiles, local_rows, local_columns, block_rows, tile_size):
    scenarios = vector.shape[1]
    gathered = lax.all_gather(vector, "row", axis=0, tiled=True)
    picked = gathered.reshape(-1, tile_size, scenarios)[local_columns]
    products = jnp.einsum("ntk,nks->nts", own_tiles, picked, preferred_element_type=jnp.float32)
    selector = (jnp.arange(block_rows, dtype=jnp.int32)[:, None] == local_rows[None, :]).astype(
        jnp.float32
    )
    partial_value = jnp.einsum("rn,nts->rts", selector, products, precision=lax.Precision.HIGHEST)
    return lax.psum_scatter(
        partial_value.reshape(-1, scenarios), "col", scatter_dimension=0, tiled=True
    )


def charge_term(vector, moved_tiles, local_rows, local_columns, block_rows, tile_size):
    scenarios = vector.shape[1]
    gathered = lax.all_gather(vector, "row", axis=0, tiled=True)
    picked = gathered.reshape(-1, tile_size, scenarios)[local_columns]
    products = jnp.einsum("nkt,nks->nts", moved_tiles, picked, preferred_element_type=jnp.float32)
    selector = (jnp.arange(block_rows, dtype=jnp.int32)[:, None] == local_rows[None, :]).astype(
        jnp.float32
    )
    partial_value = jnp.einsum("rn,nts->rts", selector, products, precision=lax.Precision.HIGHEST)
    return lax.psum_scatter(
        partial_value.reshape(-1, scenarios), "col", scatter_dimension=0, tiled=True
    )


def shards(tiles, positions, demand, value_added, extracted):
    row_devices = lax.axis_size("row")
    column_devices = lax.axis_size("col")
    row_index = lax.axis_index("row")
    column_index = lax.axis_index("col")
    tile_size = tiles.shape[-1]
    slot_count = tiles.shape[2]
    own_tiles = tiles.reshape(slot_count, tile_size, tile_size)
    scenarios = demand.shape[1]
    quarter = demand.shape[0] // tile_size
    block_rows = quarter * column_devices
    capacity = slot_count // (row_devices * column_devices)
    slot_index = jnp.arange(slot_count, dtype=jnp.int32)
    target = slot_index // capacity
    own_places = lax.dynamic_slice(
        positions, (row_index, column_index, 0), (1, 1, slot_count)
    ).reshape(slot_count)
    local_rows = target % column_devices * quarter + own_places // quarter
    local_columns = target // column_devices * quarter + own_places % quarter
    first_block = row_index * block_rows + column_index * quarter
    blocks = first_block + jnp.arange(quarter, dtype=jnp.int32)
    keep_mask = (blocks[:, None] % GROUPS != extracted[None, :]).astype(jnp.float32)[:, None, :]
    quantity = (
        keep_mask * demand.reshape(quarter, tile_size, scenarios).astype(jnp.float32)
    ).reshape(-1, scenarios)
    move = quantity.astype(jnp.bfloat16)
    for term_number in range(TERMS):
        image = supply_term(move, own_tiles, local_rows, local_columns, block_rows, tile_size)
        masked = (keep_mask * image.reshape(quarter, tile_size, scenarios)).reshape(-1, scenarios)
        quantity = quantity + masked
        if term_number + 1 < TERMS:
            move = masked.astype(jnp.bfloat16)
    price = (
        keep_mask * value_added.reshape(quarter, tile_size, scenarios).astype(jnp.float32)
    ).reshape(-1, scenarios)
    charge = price.astype(jnp.bfloat16)
    moved_tiles = lax.all_to_all(own_tiles, ("row", "col"), split_axis=0, concat_axis=0, tiled=True)
    self_index = row_index * column_devices + column_index
    table = positions.reshape(row_devices * column_devices, slot_count)
    arrived = lax.dynamic_slice_in_dim(table, self_index * capacity, capacity, axis=1).reshape(
        slot_count
    )
    source_row = target // column_devices
    source_column = target % column_devices
    moved_rows = source_column * quarter + arrived % quarter
    moved_columns = source_row * quarter + arrived // quarter
    for term_number in range(TERMS):
        cost_image = charge_term(
            charge, moved_tiles, moved_rows, moved_columns, block_rows, tile_size
        )
        masked = (keep_mask * cost_image.reshape(quarter, tile_size, scenarios)).reshape(
            -1, scenarios
        )
        price = price + masked
        if term_number + 1 < TERMS:
            charge = masked.astype(jnp.bfloat16)
    return (quantity, price)


def solution(mesh):
    placed = (
        P("row", "col", None, None, None),
        P(),
        P(("row", "col"), None),
        P(("row", "col"), None),
        P(),
    )
    return jax.shard_map(
        shards,
        mesh=mesh,
        in_specs=placed,
        out_specs=(P(("row", "col"), None), P(("row", "col"), None)),
        check_vma=False,
    )
```

profile of v0, /device:TPU:0, one launch (start us, length us, event | category | flops | bytes accessed | tf_op | source)
XLA Modules:
  0.0 448.6 jit_solution(699449108784459341)
XLA Ops:
  7.2 0.7 compare_convert_fusion
  8.0 1.7 fusion.14
  9.7 7.4 %all-to-all-start = ((bf16[64,128,128]{2,1,0:T(8,128)(2,1)}), bf16[64,128,128]{2,1,0:T(8,128)(2,1)}, u32[]{:S(2)}, u32[]{:S(2)}) async-start(bf16[64,128,128]{2,1,0:T(8,128)(2,1)} %bitcast.112), calls=%async_computation.3 | async-start | bytes 4194304 | tf_op jit(solution)/shard_map/all_to_all | solution.py:74
  18.0 51.4 %all-gather.7.cloned.1.call-done = bf16[4096,128]{1,0:T(8,128)(2,1)} async-done(((bf16[512,128]{1,0:T(8,128)(2,1)}), bf16[4096,128]{1,0:T(8,128)(2,1)}) %all-gather.7.cloned.1.call-update) | async-done | bytes 1048592 | tf_op jit(solution)/shard_map/all_gather | solution.py:12
  69.4 3.6 gather_fusion
  73.0 5.1 %fusion.49 = f32[64,128,128]{2,1,0:T(8,128)} fusion(bf16[64,128,128]{2,1,0:T(8,128)(2,1)} %gather_fusion, bf16[1,1,64,128,128]{4,3,2,1,0:T(8,128)(2,1)S(1)} %copy-done), kind=kOutput, calls=%fused_computation.99 | convolution fusion | flops 268435456 | bytes 8388608 | tf_op jit(solution)/shard_map/ntk,nks->nts/dot_general | solution.py:14
  78.2 5.4 %copy.13 = f32[64,128,128]{1,0,2:T(8,128)} copy(f32[64,128,128]{2,1,0:T(8,128)} %fusion.49) | data formatting | bytes 8388608 | tf_op jit(solution)/shard_map/ntk,nks->nts/dot_general | solution.py:14
  83.5 3.7 fusion.10
  87.2 1.3 copy.7
  88.9 21.0 %all-gather.13.cloned.1.call-done = bf16[4096,128]{1,0:T(8,128)(2,1)} async-done(((bf16[512,128]{1,0:T(8,128)(2,1)}), bf16[4096,128]{1,0:T(8,128)(2,1)}) %all-gather.13.cloned.1.call-update) | async-done | bytes 1048592 | tf_op jit(solution)/shard_map/all_gather | solution.py:26
  109.9 3.4 gather_fusion.3
  113.3 5.1 %fusion.51 = f32[64,128,128]{2,1,0:T(8,128)} fusion(bf16[64,128,128]{2,1,0:T(8,128)(2,1)} %gather_fusion.3, bf16[64,128,128]{2,1,0:T(8,128)(2,1)} %all-to-all-done), kind=kOutput, calls=%fused_computation.101 | convolution fusion | flops 268435456 | bytes 8388608 | tf_op jit(solution)/shard_map/nkt,nks->nts/dot_general | solution.py:28
  118.4 5.5 %copy.16 = f32[64,128,128]{1,0,2:T(8,128)} copy(f32[64,128,128]{2,1,0:T(8,128)} %fusion.51) | data formatting | bytes 8388608 | tf_op jit(solution)/shard_map/nkt,nks->nts/dot_general | solution.py:28
  123.9 3.7 fusion.4
  127.5 1.3 copy.10
  128.9 7.2 %reduce-scatter.7.cloned.1.call-done = f32[512,128]{1,0:T(8,128)} async-done(((f32[2048,128]{1,0:T(8,128)}), f32[512,128]{1,0:T(8,128)}) %reduce-scatter.7.cloned.1.call-update) | async-done | bytes 262160 | tf_op jit(solution)/shard_map/reduce_scatter | solution.py:19
  136.1 27.5 %reduce-scatter.13.cloned.1.call-done = f32[512,128]{1,0:T(8,128)} async-done(((f32[2048,128]{1,0:T(8,128)}), f32[512,128]{1,0:T(8,128)}) %reduce-scatter.13.cloned.1.call-update) | async-done | bytes 262160 | tf_op jit(solution)/shard_map/reduce_scatter | solution.py:33
  163.6 1.8 fusion.18
  166.2 40.1 %all-gather.15.cloned.1.call-done = bf16[4096,128]{1,0:T(8,128)(2,1)} async-done(((bf16[512,128]{1,0:T(8,128)(2,1)}), bf16[4096,128]{1,0:T(8,128)(2,1)}) %all-gather.15.cloned.1.call-update) | async-done | bytes 1048592 | tf_op jit(solution)/shard_map/all_gather | solution.py:26
  206.3 3.4 gather_fusion.4
  209.7 5.1 %fusion.52 = f32[64,128,128]{2,1,0:T(8,128)} fusion(bf16[64,128,128]{2,1,0:T(8,128)(2,1)} %gather_fusion.4, bf16[64,128,128]{2,1,0:T(8,128)(2,1)} %all-to-all-done), kind=kOutput, calls=%fused_computation.102 | convolution fusion | flops 268435456 | bytes 8388608 | tf_op jit(solution)/shard_map/nkt,nks->nts/dot_general | solution.py:28
  214.8 5.4 %copy.17 = f32[64,128,128]{1,0,2:T(8,128)} copy(f32[64,128,128]{2,1,0:T(8,128)} %fusion.52) | data formatting | bytes 8388608 | tf_op jit(solution)/shard_map/nkt,nks->nts/dot_general | solution.py:28
  220.2 3.7 fusion.2
  223.9 1.3 copy.11
  225.3 22.5 %all-gather.9.cloned.1.call-done = bf16[4096,128]{1,0:T(8,128)(2,1)} async-done(((bf16[512,128]{1,0:T(8,128)(2,1)}), bf16[4096,128]{1,0:T(8,128)(2,1)}) %all-gather.9.cloned.1.call-update) | async-done | bytes 1048592 | tf_op jit(solution)/shard_map/all_gather | solution.py:12
  247.8 3.4 gather_fusion.1
  251.2 5.2 %fusion.47 = f32[64,128,128]{2,1,0:T(8,128)} fusion(bf16[64,128,128]{2,1,0:T(8,128)(2,1)} %gather_fusion.1, bf16[1,1,64,128,128]{4,3,2,1,0:T(8,128)(2,1)S(1)} %copy-done), kind=kOutput, calls=%fused_computation.97 | convolution fusion | flops 268435456 | bytes 8388608 | tf_op jit(solution)/shard_map/ntk,nks->nts/dot_general | solution.py:14
  256.4 5.5 %copy.14 = f32[64,128,128]{1,0,2:T(8,128)} copy(f32[64,128,128]{2,1,0:T(8,128)} %fusion.47) | data formatting | bytes 8388608 | tf_op jit(solution)/shard_map/ntk,nks->nts/dot_general | solution.py:14
  261.9 3.7 fusion.8
  265.5 1.3 copy.8
  266.9 7.1 %reduce-scatter.15.cloned.1.call-done = f32[512,128]{1,0:T(8,128)} async-done(((f32[2048,128]{1,0:T(8,128)}), f32[512,128]{1,0:T(8,128)}) %reduce-scatter.15.cloned.1.call-update) | async-done | bytes 262160 | tf_op jit(solution)/shard_map/reduce_scatter | solution.py:33
  274.1 27.6 %reduce-scatter.9.cloned.1.call-done = f32[512,128]{1,0:T(8,128)} async-done(((f32[2048,128]{1,0:T(8,128)}), f32[512,128]{1,0:T(8,128)}) %reduce-scatter.9.cloned.1.call-update) | async-done | bytes 262160 | tf_op jit(solution)/shard_map/reduce_scatter | solution.py:19
  301.7 1.8 fusion.19
  304.1 40.5 %all-gather.17.cloned.1.call-done = bf16[4096,128]{1,0:T(8,128)(2,1)} async-done(((bf16[512,128]{1,0:T(8,128)(2,1)}), bf16[4096,128]{1,0:T(8,128)(2,1)}) %all-gather.17.cloned.1.call-update) | async-done | bytes 1048592 | tf_op jit(solution)/shard_map/all_gather | solution.py:26
  344.6 3.4 gather_fusion.5
  348.0 5.1 %fusion.53 = f32[64,128,128]{2,1,0:T(8,128)} fusion(bf16[64,128,128]{2,1,0:T(8,128)(2,1)} %gather_fusion.5, bf16[64,128,128]{2,1,0:T(8,128)(2,1)} %all-to-all-done), kind=kOutput, calls=%fused_computation.103 | convolution fusion | flops 268435456 | bytes 8388608 | tf_op jit(solution)/shard_map/nkt,nks->nts/dot_general | solution.py:28
  353.1 5.4 %copy.18 = f32[64,128,128]{1,0,2:T(8,128)} copy(f32[64,128,128]{2,1,0:T(8,128)} %fusion.53) | data formatting | bytes 8388608 | tf_op jit(solution)/shard_map/nkt,nks->nts/dot_general | solution.py:28
  358.5 3.7 fusion
  362.2 1.4 copy.12
  363.8 22.2 %all-gather.11.cloned.1.call-done = bf16[4096,128]{1,0:T(8,128)(2,1)} async-done(((bf16[512,128]{1,0:T(8,128)(2,1)}), bf16[4096,128]{1,0:T(8,128)(2,1)}) %all-gather.11.cloned.1.call-update) | async-done | bytes 1048592 | tf_op jit(solution)/shard_map/all_gather | solution.py:12
  386.1 3.4 gather_fusion.2
  389.5 5.2 %fusion.45 = f32[64,128,128]{2,1,0:T(8,128)} fusion(bf16[64,128,128]{2,1,0:T(8,128)(2,1)} %gather_fusion.2, bf16[1,1,64,128,128]{4,3,2,1,0:T(8,128)(2,1)S(1)} %copy-done), kind=kOutput, calls=%fused_computation.95 | convolution fusion | flops 268435456 | bytes 8388608 | tf_op jit(solution)/shard_map/ntk,nks->nts/dot_general | solution.py:14
  394.7 5.4 %copy.15 = f32[64,128,128]{1,0,2:T(8,128)} copy(f32[64,128,128]{2,1,0:T(8,128)} %fusion.45) | data formatting | bytes 8388608 | tf_op jit(solution)/shard_map/ntk,nks->nts/dot_general | solution.py:14
  400.1 3.6 fusion.6
  403.8 1.3 copy.9
  405.1 7.1 %reduce-scatter.17.cloned.1.call-done = f32[512,128]{1,0:T(8,128)} async-done(((f32[2048,128]{1,0:T(8,128)}), f32[512,128]{1,0:T(8,128)}) %reduce-scatter.17.cloned.1.call-update) | async-done | bytes 262160 | tf_op jit(solution)/shard_map/reduce_scatter | solution.py:33
  412.2 27.5 %reduce-scatter.11.cloned.1.call-done = f32[512,128]{1,0:T(8,128)} async-done(((f32[2048,128]{1,0:T(8,128)}), f32[512,128]{1,0:T(8,128)}) %reduce-scatter.11.cloned.1.call-update) | async-done | bytes 262160 | tf_op jit(solution)/shard_map/reduce_scatter | solution.py:19
  439.8 2.0 fusion.13
  (51 shorter events, 3.2 us)
Async XLA Ops:
  7.2 62.3 %all-gather.7.cloned.1.call-start = ((), (), s32[]{:S(2)}) async-start(), calls=%async_computation.7 | async-start | bytes 1179648 | tf_op jit(solution)/shard_map/all_gather | solution.py:12
  9.7 8.3 %copy-start.7 = (s32[8,4,64]{2,1,0:T(4,128)S(1)}, s32[8,4,64]{2,1,0:T(4,128)}, u32[]{:S(2)}) copy-start(s32[8,4,64]{2,1,0:T(4,128)} %param.6) | copy-start | bytes 24580
  9.7 103.6 %all-to-all-start = ((bf16[64,128,128]{2,1,0:T(8,128)(2,1)}), bf16[64,128,128]{2,1,0:T(8,128)(2,1)}, u32[]{:S(2)}, u32[]{:S(2)}) async-start(bf16[64,128,128]{2,1,0:T(8,128)(2,1)} %bitcast.112), calls=%async_computation.3 | async-start | bytes 4194304 | tf_op jit(solution)/shard_map/all_to_all | solution.py:74
  17.2 92.8 %all-gather.13.cloned.1.call-start = ((), (), s32[]{:S(2)}) async-start(), calls=%async_computation.13 | async-start | bytes 1179648 | tf_op jit(solution)/shard_map/all_gather | solution.py:26
  17.9 118.2 %reduce-scatter.7.cloned.1.call-start = ((), (), s32[]{:S(2)}) async-start(), calls=%async_computation.8 | async-start | bytes 1310720 | tf_op jit(solution)/shard_map/reduce_scatter | solution.py:19
  69.4 3.6 copy-start
  88.5 75.1 %reduce-scatter.13.cloned.1.call-start = ((), (), s32[]{:S(2)}) async-start(), calls=%async_computation.14 | async-start | bytes 1310720 | tf_op jit(solution)/shard_map/reduce_scatter | solution.py:33
  128.9 77.5 %all-gather.15.cloned.1.call-start = ((), (), s32[]{:S(2)}) async-start(), calls=%async_computation.15 | async-start | bytes 1179648 | tf_op jit(solution)/shard_map/all_gather | solution.py:26
  165.4 82.4 %all-gather.9.cloned.1.call-start = ((), (), s32[]{:S(2)}) async-start(), calls=%async_computation.9 | async-start | bytes 1179648 | tf_op jit(solution)/shard_map/all_gather | solution.py:12
  166.0 108.1 %reduce-scatter.15.cloned.1.call-start = ((), (), s32[]{:S(2)}) async-start(), calls=%async_computation.16 | async-start | bytes 1310720 | tf_op jit(solution)/shard_map/reduce_scatter | solution.py:33
  225.3 76.4 %reduce-scatter.9.cloned.1.call-start = ((), (), s32[]{:S(2)}) async-start(), calls=%async_computation.10 | async-start | bytes 1310720 | tf_op jit(solution)/shard_map/reduce_scatter | solution.py:19
  266.9 77.7 %all-gather.17.cloned.1.call-start = ((), (), s32[]{:S(2)}) async-start(), calls=%async_computation.17 | async-start | bytes 1179648 | tf_op jit(solution)/shard_map/all_gather | solution.py:26
  303.5 82.6 %all-gather.11.cloned.1.call-start = ((), (), s32[]{:S(2)}) async-start(), calls=%async_computation.11 | async-start | bytes 1179648 | tf_op jit(solution)/shard_map/all_gather | solution.py:12
  304.1 108.2 %reduce-scatter.17.cloned.1.call-start = ((), (), s32[]{:S(2)}) async-start(), calls=%async_computation.18 | async-start | bytes 1310720 | tf_op jit(solution)/shard_map/reduce_scatter | solution.py:33
  363.6 76.2 %reduce-scatter.11.cloned.1.call-start = ((), (), s32[]{:S(2)}) async-start(), calls=%async_computation.12 | async-start | bytes 1310720 | tf_op jit(solution)/shard_map/reduce_scatter | solution.py:19
  403.7 36.0 %copy-start.1 = (f32[512,128]{1,0:T(8,128)S(1)}, f32[512,128]{1,0:T(8,128)}, u32[]{:S(2)}) copy-start(f32[512,128]{1,0:T(8,128)} %reduce-scatter.7.cloned.1.call-done) | copy-start | bytes 786436
  403.8 36.0 %copy-start.2 = (f32[512,128]{1,0:T(8,128)S(1)}, f32[512,128]{1,0:T(8,128)}, u32[]{:S(2)}) copy-start(f32[512,128]{1,0:T(8,128)} %reduce-scatter.13.cloned.1.call-done) | copy-start | bytes 786436
  403.8 36.0 %copy-start.3 = (f32[512,128]{1,0:T(8,128)S(1)}, f32[512,128]{1,0:T(8,128)}, u32[]{:S(2)}) copy-start(f32[512,128]{1,0:T(8,128)} %reduce-scatter.15.cloned.1.call-done) | copy-start | bytes 786436
  403.8 36.0 %copy-start.4 = (f32[512,128]{1,0:T(8,128)S(1)}, f32[512,128]{1,0:T(8,128)}, u32[]{:S(2)}) copy-start(f32[512,128]{1,0:T(8,128)} %reduce-scatter.9.cloned.1.call-done) | copy-start | bytes 786436
  403.8 36.0 %copy-start.5 = (bf16[512,128]{1,0:T(8,128)(2,1)S(1)}, bf16[512,128]{1,0:T(8,128)(2,1)}, u32[]{:S(2)}) copy-start(bf16[512,128]{1,0:T(8,128)(2,1)} %param.8) | copy-start | bytes 393220
  403.8 36.0 %copy-start.6 = (bf16[512,128]{1,0:T(8,128)(2,1)S(1)}, bf16[512,128]{1,0:T(8,128)(2,1)}, u32[]{:S(2)}) copy-start(bf16[512,128]{1,0:T(8,128)(2,1)} %param.7) | copy-start | bytes 393220
Sparse Core Ops, SparseCore 0:
  10.7 58.6 all-gather.6
  72.1 37.7 all-gather.12
  112.5 23.6 reduce-scatter.6
  138.7 24.8 reduce-scatter.12
  166.2 40.1 all-gather.14
  208.9 38.8 all-gather.8
  250.4 23.6 reduce-scatter.14
  276.7 24.8 reduce-scatter.8
  304.4 40.1 all-gather.16
  347.1 38.8 all-gather.10
  388.6 23.6 reduce-scatter.16
  414.8 24.8 reduce-scatter.10
where the time goes:
time: 450 us; the launch traced here: 449 us
  waiting for transfers between devices  304 us (68%)
  local copies, waits for them, and re-layouts  61.3 us (14%)
  matrix products  52.8 us (12%)
  between operations  14.4 us (3%)
  starting transfers between devices  8.32 us (2%)
  other arithmetic  8.04 us (2%)
    all_gather x3, waiting for transfers between devices, charge_term(): gathered = lax.all_gather(vector, 'row', axis=0, tiled=True)  102 us
    all_gather x3, waiting for transfers between devices, supply_term(): gathered = lax.all_gather(vector, 'row', axis=0, tiled=True)  96.2 us
    reduce_scatter x3, waiting for transfers between devices, supply_term(): lax.psum_scatter(partial_value.reshape(-1, scenarios), 'col', scatter_dim...  62.3 us
    reduce_scatter x3, waiting for transfers between devices, charge_term(): lax.psum_scatter(partial_value.reshape(-1, scenarios), 'col', scatter_dim...  41.7 us
    dot_general x3, local copies, waits for them, and re-layouts, charge_term(): jnp.einsum('nkt,nks->nts', moved_tiles, picked, preferred_element_type=jn...  16.3 us
    dot_general x3, local copies, waits for them, and re-layouts, supply_term(): jnp.einsum('ntk,nks->nts', own_tiles, picked, preferred_element_type=jnp....  16.3 us
    dot_general x3, matrix products, supply_term(): jnp.einsum('ntk,nks->nts', own_tiles, picked, preferred_element_type=jnp....  15.5 us
    dot_general x3, matrix products, charge_term(): jnp.einsum('nkt,nks->nts', moved_tiles, picked, preferred_element_type=jn...  15.3 us
  transfers between devices with their start and end apart: 13, of which 12 were waited for; matrix products, arithmetic and copies ran while one was open for 25% of the time, Pallas kernels for 0%

commit v1 on v0

--- a/solution.py
+++ b/solution.py
@@ -9,7 +9,16 @@
 
 def supply_term(vector, own_tiles, local_rows, local_columns, block_rows, tile_size):
     scenarios = vector.shape[1]
-    gathered = lax.all_gather(vector, "row", axis=0, tiled=True)
+    everything, block_next = (lax.axis_size("row"), lax.axis_index("row"))
+    gathered, local_part = (vector, 1)
+    while local_part < everything:
+        d_next = lax.ppermute(
+            gathered, "row", tuple(((dev_j, dev_j ^ local_part) for dev_j in range(everything)))
+        )
+        extra = jnp.concatenate([gathered, d_next], 0)
+        newest = jnp.concatenate([d_next, gathered], 0)
+        gathered = jnp.where(block_next & local_part == 0, extra, newest)
+        local_part = 2 * local_part
     picked = gathered.reshape(-1, tile_size, scenarios)[local_columns]
     products = jnp.einsum("ntk,nks->nts", own_tiles, picked, preferred_element_type=jnp.float32)
     selector = (jnp.arange(block_rows, dtype=jnp.int32)[:, None] == local_rows[None, :]).astype(

time: 450 us -> 405 us (0.900)
  waiting for transfers between devices: 304 us -> 246 us
  starting transfers between devices: 8.32 us -> 25.6 us
  local copies, waits for them, and re-layouts: 61.3 us -> 56.2 us
    ppermute x0 -> x9, waiting for transfers between devices: none -> 146 us  [supply_term(): lax.ppermute(gathered, 'row', tuple(((dev_j, dev_j ^ local_part) for dev_...]
    all_gather x3 -> x0, waiting for transfers between devices: 96.2 us -> none  [supply_term(): gathered = lax.all_gather(vector, 'row', axis=0, tiled=True)]
    all_gather x3, waiting for transfers between devices: 102 us -> 5.97 us  [charge_term(): gathered = lax.all_gather(vector, 'row', axis=0, tiled=True)]
    reduce_scatter x3, waiting for transfers between devices: 62.3 us -> 12.2 us  [supply_term(): lax.psum_scatter(partial_value.reshape(-1, scenarios), 'col', scatter_dim...]
    reduce_scatter x3, waiting for transfers between devices: 41.7 us -> 82.5 us  [charge_term(): lax.psum_scatter(partial_value.reshape(-1, scenarios), 'col', scatter_dim...]
    ppermute x0 -> x9, starting transfers between devices: none -> 17.3 us  [supply_term(): lax.ppermute(gathered, 'row', tuple(((dev_j, dev_j ^ local_part) for dev_...]
  transfers between devices with their start and end apart: 13 -> 19, of which waited for: 12 -> 17; matrix products, arithmetic and copies ran while one was open for 25% -> 27% of each run, Pallas kernels for 0% -> 0%
where the time goes in v1:
time: 405 us; the launch traced here: 404 us
  waiting for transfers between devices  246 us (61%)
  local copies, waits for them, and re-layouts  56.2 us (14%)
  matrix products  52.8 us (13%)
  starting transfers between devices  25.6 us (6%)
  between operations  15.5 us (4%)
  other arithmetic  7.77 us (2%)
    ppermute x9, waiting for transfers between devices, supply_term(): lax.ppermute(gathered, 'row', tuple(((dev_j, dev_j ^ local_part) for dev_...  146 us
    reduce_scatter x3, waiting for transfers between devices, charge_term(): lax.psum_scatter(partial_value.reshape(-1, scenarios), 'col', scatter_dim...  82.5 us
    ppermute x9, starting transfers between devices, supply_term(): lax.ppermute(gathered, 'row', tuple(((dev_j, dev_j ^ local_part) for dev_...  17.3 us
    dot_general x3, local copies, waits for them, and re-layouts, supply_term(): jnp.einsum('ntk,nks->nts', own_tiles, picked, preferred_element_type=jnp....  16.2 us
    dot_general x3, local copies, waits for them, and re-layouts, charge_term(): jnp.einsum('nkt,nks->nts', moved_tiles, picked, preferred_element_type=jn...  16.2 us
    dot_general x3, matrix products, supply_term(): jnp.einsum('ntk,nks->nts', own_tiles, picked, preferred_element_type=jnp....  15.5 us
    dot_general x3, matrix products, charge_term(): jnp.einsum('nkt,nks->nts', moved_tiles, picked, preferred_element_type=jn...  14.9 us
    reduce_scatter x3, waiting for transfers between devices, supply_term(): lax.psum_scatter(partial_value.reshape(-1, scenarios), 'col', scatter_dim...  12.2 us
  transfers between devices with their start and end apart: 19, of which 17 were waited for; matrix products, arithmetic and copies ran while one was open for 27% of the time, Pallas kernels for 0%

profile of v1, /device:TPU:0, one launch (start us, length us, event | category | flops | bytes accessed | tf_op | source)
XLA Modules:
  0.0 404.3 jit_solution(9604293863486950648)
XLA Ops:
  8.0 7.4 %all-to-all-start = ((bf16[64,128,128]{2,1,0:T(8,128)(2,1)}), bf16[64,128,128]{2,1,0:T(8,128)(2,1)}, u32[]{:S(2)}, u32[]{:S(2)}) async-start(bf16[64,128,128]{2,1,0:T(8,128)(2,1)} %bitcast.112), calls=%async_computation.3 | async-start | bytes 4194304 | tf_op jit(solution)/shard_map/all_to_all | solution.py:83
  18.0 18.0 %collective-permute-done = bf16[512,128]{1,0:T(8,128)(2,1)S(1)} collective-permute-done((bf16[512,128]{1,0:T(8,128)(2,1)S(1)}, bf16[512,128]{1,0:T(8,128)(2,1)S(1)}, u32[]{:S(2)}, u32[]{:S(2)}) %collective-permute-start) | collective-permute-done | bytes 131104 | tf_op jit(solution)/shard_map/ppermute | solution.py:15
  36.3 23.5 %collective-permute-done.1 = bf16[1024,128]{1,0:T(8,128)(2,1)S(1)} collective-permute-done((bf16[1024,128]{1,0:T(8,128)(2,1)S(1)}, bf16[1024,128]{1,0:T(8,128)(2,1)S(1)}, u32[]{:S(2)}, u32[]{:S(2)}) %collective-permute-start.1) | collective-permute-done | bytes 262176 | tf_op jit(solution)/shard_map/ppermute | solution.py:15
  59.9 4.6 %collective-permute-start.2 = (bf16[2048,128]{1,0:T(8,128)(2,1)S(1)}, bf16[2048,128]{1,0:T(8,128)(2,1)S(1)}, u32[]{:S(2)}, u32[]{:S(2)}) collective-permute-start(bf16[2048,128]{1,0:T(8,128)(2,1)S(1)} %maximum_select_fusion.3), channel_id=1, source_target_pairs={{0,16},{4,20},{8,24},{12,28},{16,0},{20,4},{24,8},{28,12},{1,17},{... | collective-permute-start | bytes 1572872 | tf_op jit(solution)/shard_map/ppermute | solution.py:15
  64.6 34.7 %collective-permute-done.2 = bf16[2048,128]{1,0:T(8,128)(2,1)S(1)} collective-permute-done((bf16[2048,128]{1,0:T(8,128)(2,1)S(1)}, bf16[2048,128]{1,0:T(8,128)(2,1)S(1)}, u32[]{:S(2)}, u32[]{:S(2)}) %collective-permute-start.2) | collective-permute-done | bytes 524320 | tf_op jit(solution)/shard_map/ppermute | solution.py:15
  99.6 2.2 gather_fusion
  101.8 5.2 %fusion.49 = f32[64,128,128]{2,1,0:T(8,128)} fusion(bf16[64,128,128]{2,1,0:T(8,128)(2,1)} %gather_fusion, bf16[1,1,64,128,128]{4,3,2,1,0:T(8,128)(2,1)S(1)} %copy-done), kind=kOutput, calls=%fused_computation.108 | convolution fusion | flops 268435456 | bytes 8388608 | tf_op jit(solution)/shard_map/ntk,nks->nts/dot_general | solution.py:23
  106.9 5.4 %copy.13 = f32[64,128,128]{1,0,2:T(8,128)} copy(f32[64,128,128]{2,1,0:T(8,128)} %fusion.49) | data formatting | bytes 8388608 | tf_op jit(solution)/shard_map/ntk,nks->nts/dot_general | solution.py:23
  112.3 3.7 fusion.10
  117.7 3.4 gather_fusion.3
  121.2 5.2 %fusion.51 = f32[64,128,128]{2,1,0:T(8,128)} fusion(bf16[64,128,128]{2,1,0:T(8,128)(2,1)} %gather_fusion.3, bf16[64,128,128]{2,1,0:T(8,128)(2,1)} %all-to-all-done), kind=kOutput, calls=%fused_computation.110 | convolution fusion | flops 268435456 | bytes 8388608 | tf_op jit(solution)/shard_map/nkt,nks->nts/dot_general | solution.py:37
  126.4 5.4 %copy.16 = f32[64,128,128]{1,0,2:T(8,128)} copy(f32[64,128,128]{2,1,0:T(8,128)} %fusion.51) | data formatting | bytes 8388608 | tf_op jit(solution)/shard_map/nkt,nks->nts/dot_general | solution.py:37
  131.8 3.8 fusion.4
  137.0 4.8 %reduce-scatter.7.cloned.1.call-done = f32[512,128]{1,0:T(8,128)} async-done(((f32[2048,128]{1,0:T(8,128)}), f32[512,128]{1,0:T(8,128)}) %reduce-scatter.7.cloned.1.call-update) | async-done | bytes 262160 | tf_op jit(solution)/shard_map/reduce_scatter | solution.py:28
  141.8 27.4 %reduce-scatter.13.cloned.1.call-done = f32[512,128]{1,0:T(8,128)} async-done(((f32[2048,128]{1,0:T(8,128)}), f32[512,128]{1,0:T(8,128)}) %reduce-scatter.13.cloned.1.call-update) | async-done | bytes 262160 | tf_op jit(solution)/shard_map/reduce_scatter | solution.py:42
  169.2 1.7 fusion.18
  172.4 3.7 collective-permute-done.3
  177.9 5.3 %collective-permute-done.4 = bf16[1024,128]{1,0:T(8,128)(2,1)S(1)} collective-permute-done((bf16[1024,128]{1,0:T(8,128)(2,1)S(1)}, bf16[1024,128]{1,0:T(8,128)(2,1)S(1)}, u32[]{:S(2)}, u32[]{:S(2)}) %collective-permute-start.4) | collective-permute-done | bytes 262176 | tf_op jit(solution)/shard_map/ppermute | solution.py:15
  183.4 2.5 collective-permute-start.5
  185.8 25.8 %collective-permute-done.5 = bf16[2048,128]{1,0:T(8,128)(2,1)S(1)} collective-permute-done((bf16[2048,128]{1,0:T(8,128)(2,1)S(1)}, bf16[2048,128]{1,0:T(8,128)(2,1)S(1)}, u32[]{:S(2)}, u32[]{:S(2)}) %collective-permute-start.5) | collective-permute-done | bytes 524320 | tf_op jit(solution)/shard_map/ppermute | solution.py:15
  211.9 2.2 gather_fusion.1
  214.1 5.2 %fusion.47 = f32[64,128,128]{2,1,0:T(8,128)} fusion(bf16[64,128,128]{2,1,0:T(8,128)(2,1)} %gather_fusion.1, bf16[1,1,64,128,128]{4,3,2,1,0:T(8,128)(2,1)S(1)} %copy-done), kind=kOutput, calls=%fused_computation.106 | convolution fusion | flops 268435456 | bytes 8388608 | tf_op jit(solution)/shard_map/ntk,nks->nts/dot_general | solution.py:23
  219.3 5.4 %copy.14 = f32[64,128,128]{1,0,2:T(8,128)} copy(f32[64,128,128]{2,1,0:T(8,128)} %fusion.47) | data formatting | bytes 8388608 | tf_op jit(solution)/shard_map/ntk,nks->nts/dot_general | solution.py:23
  224.7 3.7 fusion.8
  229.7 3.0 all-gather.6.cloned.1.call-done
  232.7 3.4 gather_fusion.4
  236.2 5.3 %fusion.52 = f32[64,128,128]{2,1,0:T(8,128)} fusion(bf16[64,128,128]{2,1,0:T(8,128)(2,1)} %gather_fusion.4, bf16[64,128,128]{2,1,0:T(8,128)(2,1)} %all-to-all-done), kind=kOutput, calls=%fused_computation.111 | convolution fusion | flops 268435456 | bytes 8388608 | tf_op jit(solution)/shard_map/nkt,nks->nts/dot_general | solution.py:37
  241.4 5.4 %copy.17 = f32[64,128,128]{1,0,2:T(8,128)} copy(f32[64,128,128]{2,1,0:T(8,128)} %fusion.52) | data formatting | bytes 8388608 | tf_op jit(solution)/shard_map/nkt,nks->nts/dot_general | solution.py:37
  246.8 3.7 fusion.2
  251.9 2.7 reduce-scatter.9.cloned.1.call-done
  254.6 27.6 %reduce-scatter.15.cloned.1.call-done = f32[512,128]{1,0:T(8,128)} async-done(((f32[2048,128]{1,0:T(8,128)}), f32[512,128]{1,0:T(8,128)}) %reduce-scatter.15.cloned.1.call-update) | async-done | bytes 262160 | tf_op jit(solution)/shard_map/reduce_scatter | solution.py:42
  282.1 1.7 fusion.19
  285.4 3.7 collective-permute-done.6
  291.0 5.3 %collective-permute-done.7 = bf16[1024,128]{1,0:T(8,128)(2,1)S(1)} collective-permute-done((bf16[1024,128]{1,0:T(8,128)(2,1)S(1)}, bf16[1024,128]{1,0:T(8,128)(2,1)S(1)}, u32[]{:S(2)}, u32[]{:S(2)}) %collective-permute-start.7) | collective-permute-done | bytes 262176 | tf_op jit(solution)/shard_map/ppermute | solution.py:15
  296.4 2.4 collective-permute-start.8
  298.8 25.9 %collective-permute-done.8 = bf16[2048,128]{1,0:T(8,128)(2,1)S(1)} collective-permute-done((bf16[2048,128]{1,0:T(8,128)(2,1)S(1)}, bf16[2048,128]{1,0:T(8,128)(2,1)S(1)}, u32[]{:S(2)}, u32[]{:S(2)}) %collective-permute-start.8) | collective-permute-done | bytes 524320 | tf_op jit(solution)/shard_map/ppermute | solution.py:15
  325.0 2.2 gather_fusion.2
  327.2 5.2 %fusion.45 = f32[64,128,128]{2,1,0:T(8,128)} fusion(bf16[64,128,128]{2,1,0:T(8,128)(2,1)} %gather_fusion.2, bf16[1,1,64,128,128]{4,3,2,1,0:T(8,128)(2,1)S(1)} %copy-done), kind=kOutput, calls=%fused_computation.104 | convolution fusion | flops 268435456 | bytes 8388608 | tf_op jit(solution)/shard_map/ntk,nks->nts/dot_general | solution.py:23
  332.3 5.4 %copy.15 = f32[64,128,128]{1,0,2:T(8,128)} copy(f32[64,128,128]{2,1,0:T(8,128)} %fusion.45) | data formatting | bytes 8388608 | tf_op jit(solution)/shard_map/ntk,nks->nts/dot_general | solution.py:23
  337.7 3.7 fusion.6
  342.8 2.9 all-gather.8.cloned.1.call-done
  345.7 2.2 gather_fusion.5
  347.9 4.4 %fusion.53 = f32[64,128,128]{2,1,0:T(8,128)} fusion(bf16[64,128,128]{2,1,0:T(8,128)(2,1)S(1)} %gather_fusion.5, bf16[64,128,128]{2,1,0:T(8,128)(2,1)} %all-to-all-done), kind=kOutput, calls=%fused_computation.112 | convolution fusion | flops 268435456 | bytes 8388608 | tf_op jit(solution)/shard_map/nkt,nks->nts/dot_general | solution.py:37
  352.3 5.4 %copy.18 = f32[64,128,128]{1,0,2:T(8,128)} copy(f32[64,128,128]{2,1,0:T(8,128)} %fusion.53) | data formatting | bytes 8388608 | tf_op jit(solution)/shard_map/nkt,nks->nts/dot_general | solution.py:37
  357.8 3.8 fusion
  363.0 4.7 %reduce-scatter.11.cloned.1.call-done = f32[512,128]{1,0:T(8,128)} async-done(((f32[2048,128]{1,0:T(8,128)}), f32[512,128]{1,0:T(8,128)}) %reduce-scatter.11.cloned.1.call-update) | async-done | bytes 262160 | tf_op jit(solution)/shard_map/reduce_scatter | solution.py:28
  367.6 27.5 %reduce-scatter.17.cloned.1.call-done = f32[512,128]{1,0:T(8,128)} async-done(((f32[2048,128]{1,0:T(8,128)}), f32[512,128]{1,0:T(8,128)}) %reduce-scatter.17.cloned.1.call-update) | async-done | bytes 262160 | tf_op jit(solution)/shard_map/reduce_scatter | solution.py:42
  395.2 2.0 fusion.13
  (71 shorter events, 19.3 us)
Async XLA Ops:
  8.0 7.6 %copy-start.8 = (s32[128]{0:T(128)S(1)}, s32[128]{0:T(128)}, u32[]{:S(2)}) copy-start(s32[128]{0:T(128)} %param.9) | copy-start | bytes 1540
  8.0 7.6 %copy-start.5 = (bf16[512,128]{1,0:T(8,128)(2,1)S(1)}, bf16[512,128]{1,0:T(8,128)(2,1)}, u32[]{:S(2)}) copy-start(bf16[512,128]{1,0:T(8,128)(2,1)} %param.8) | copy-start | bytes 393220
  8.0 7.6 %copy-start.6 = (bf16[512,128]{1,0:T(8,128)(2,1)S(1)}, bf16[512,128]{1,0:T(8,128)(2,1)}, u32[]{:S(2)}) copy-start(bf16[512,128]{1,0:T(8,128)(2,1)} %param.7) | copy-start | bytes 393220
  8.0 113.1 %all-to-all-start = ((bf16[64,128,128]{2,1,0:T(8,128)(2,1)}), bf16[64,128,128]{2,1,0:T(8,128)(2,1)}, u32[]{:S(2)}, u32[]{:S(2)}) async-start(bf16[64,128,128]{2,1,0:T(8,128)(2,1)} %bitcast.112), calls=%async_computation.3 | async-start | bytes 4194304 | tf_op jit(solution)/shard_map/all_to_all | solution.py:83
  15.5 49.1 %copy-start.7 = (s32[8,4,64]{2,1,0:T(4,128)S(1)}, s32[8,4,64]{2,1,0:T(4,128)}, u32[]{:S(2)}) copy-start(s32[8,4,64]{2,1,0:T(4,128)} %param.6) | copy-start | bytes 24580
  15.5 102.3 %all-gather.4.cloned.1.call-start = ((), (), s32[]{:S(2)}) async-start(), calls=%async_computation.10 | async-start | bytes 1179648 | tf_op jit(solution)/shard_map/all_gather | solution.py:35
  16.3 19.7 %collective-permute-start = (bf16[512,128]{1,0:T(8,128)(2,1)S(1)}, bf16[512,128]{1,0:T(8,128)(2,1)S(1)}, u32[]{:S(2)}, u32[]{:S(2)}) collective-permute-start(bf16[512,128]{1,0:T(8,128)(2,1)S(1)} %get-tuple-element.9), channel_id=1, source_target_pairs={{0,4},{4,0},{8,12},{12,8},{16,20},{20,16},{24,28},{28,24},{1,5},{5... | collective-permute-start | bytes 393224 | tf_op jit(solution)/shard_map/ppermute | solution.py:15
  36.1 23.7 %collective-permute-start.1 = (bf16[1024,128]{1,0:T(8,128)(2,1)S(1)}, bf16[1024,128]{1,0:T(8,128)(2,1)S(1)}, u32[]{:S(2)}, u32[]{:S(2)}) collective-permute-start(bf16[1024,128]{1,0:T(8,128)(2,1)S(1)} %maximum_select_fusion.6), channel_id=1, source_target_pairs={{0,8},{4,12},{8,0},{12,4},{16,24},{20,28},{24,16},{28,20},{1,9},{5... | collective-permute-start | bytes 786440 | tf_op jit(solution)/shard_map/ppermute | solution.py:15
  36.2 105.6 %reduce-scatter.7.cloned.1.call-start = ((), (), s32[]{:S(2)}) async-start(), calls=%async_computation.7 | async-start | bytes 1310720 | tf_op jit(solution)/shard_map/reduce_scatter | solution.py:28
  59.9 39.4 %collective-permute-start.2 = (bf16[2048,128]{1,0:T(8,128)(2,1)S(1)}, bf16[2048,128]{1,0:T(8,128)(2,1)S(1)}, u32[]{:S(2)}, u32[]{:S(2)}) collective-permute-start(bf16[2048,128]{1,0:T(8,128)(2,1)S(1)} %maximum_select_fusion.3), channel_id=1, source_target_pairs={{0,16},{4,20},{8,24},{12,28},{16,0},{20,4},{24,8},{28,12},{1,17},{... | collective-permute-start | bytes 1572872 | tf_op jit(solution)/shard_map/ppermute | solution.py:15
  99.5 2.2 copy-start
  117.3 51.9 %reduce-scatter.13.cloned.1.call-start = ((), (), s32[]{:S(2)}) async-start(), calls=%async_computation.11 | async-start | bytes 1310720 | tf_op jit(solution)/shard_map/reduce_scatter | solution.py:42
  137.0 95.8 %all-gather.6.cloned.1.call-start = ((), (), s32[]{:S(2)}) async-start(), calls=%async_computation.12 | async-start | bytes 1179648 | tf_op jit(solution)/shard_map/all_gather | solution.py:35
  170.9 5.1 %collective-permute-start.3 = (bf16[512,128]{1,0:T(8,128)(2,1)S(1)}, bf16[512,128]{1,0:T(8,128)(2,1)S(1)}, u32[]{:S(2)}, u32[]{:S(2)}) collective-permute-start(bf16[512,128]{1,0:T(8,128)(2,1)S(1)} %get-tuple-element.7), channel_id=1, source_target_pairs={{0,4},{4,0},{8,12},{12,8},{16,20},{20,16},{24,28},{28,24},{1,5},{5... | collective-permute-start | bytes 393224 | tf_op jit(solution)/shard_map/ppermute | solution.py:15
  176.1 7.1 %collective-permute-start.4 = (bf16[1024,128]{1,0:T(8,128)(2,1)S(1)}, bf16[1024,128]{1,0:T(8,128)(2,1)S(1)}, u32[]{:S(2)}, u32[]{:S(2)}) collective-permute-start(bf16[1024,128]{1,0:T(8,128)(2,1)S(1)} %maximum_select_fusion.7), channel_id=1, source_target_pairs={{0,8},{4,12},{8,0},{12,4},{16,24},{20,28},{24,16},{28,20},{1,9},{5... | collective-permute-start | bytes 786440 | tf_op jit(solution)/shard_map/ppermute | solution.py:15
  177.7 76.9 %reduce-scatter.9.cloned.1.call-start = ((), (), s32[]{:S(2)}) async-start(), calls=%async_computation.8 | async-start | bytes 1310720 | tf_op jit(solution)/shard_map/reduce_scatter | solution.py:28
  183.4 28.3 %collective-permute-start.5 = (bf16[2048,128]{1,0:T(8,128)(2,1)S(1)}, bf16[2048,128]{1,0:T(8,128)(2,1)S(1)}, u32[]{:S(2)}, u32[]{:S(2)}) collective-permute-start(bf16[2048,128]{1,0:T(8,128)(2,1)S(1)} %maximum_select_fusion.4), channel_id=1, source_target_pairs={{0,16},{4,20},{8,24},{12,28},{16,0},{20,4},{24,8},{28,12},{1,17},{... | collective-permute-start | bytes 1572872 | tf_op jit(solution)/shard_map/ppermute | solution.py:15
  229.7 52.5 %reduce-scatter.15.cloned.1.call-start = ((), (), s32[]{:S(2)}) async-start(), calls=%async_computation.13 | async-start | bytes 1310720 | tf_op jit(solution)/shard_map/reduce_scatter | solution.py:42
  251.8 93.9 %all-gather.8.cloned.1.call-start = ((), (), s32[]{:S(2)}) async-start(), calls=%async_computation.14 | async-start | bytes 1179648 | tf_op jit(solution)/shard_map/all_gather | solution.py:35
  283.9 5.2 %collective-permute-start.6 = (bf16[512,128]{1,0:T(8,128)(2,1)S(1)}, bf16[512,128]{1,0:T(8,128)(2,1)S(1)}, u32[]{:S(2)}, u32[]{:S(2)}) collective-permute-start(bf16[512,128]{1,0:T(8,128)(2,1)S(1)} %get-tuple-element.5), channel_id=1, source_target_pairs={{0,4},{4,0},{8,12},{12,8},{16,20},{20,16},{24,28},{28,24},{1,5},{5... | collective-permute-start | bytes 393224 | tf_op jit(solution)/shard_map/ppermute | solution.py:15
  289.1 7.1 %collective-permute-start.7 = (bf16[1024,128]{1,0:T(8,128)(2,1)S(1)}, bf16[1024,128]{1,0:T(8,128)(2,1)S(1)}, u32[]{:S(2)}, u32[]{:S(2)}) collective-permute-start(bf16[1024,128]{1,0:T(8,128)(2,1)S(1)} %maximum_select_fusion.8), channel_id=1, source_target_pairs={{0,8},{4,12},{8,0},{12,4},{16,24},{20,28},{24,16},{28,20},{1,9},{5... | collective-permute-start | bytes 786440 | tf_op jit(solution)/shard_map/ppermute | solution.py:15
  290.7 76.9 %reduce-scatter.11.cloned.1.call-start = ((), (), s32[]{:S(2)}) async-start(), calls=%async_computation.9 | async-start | bytes 1310720 | tf_op jit(solution)/shard_map/reduce_scatter | solution.py:28
  296.4 28.3 %collective-permute-start.8 = (bf16[2048,128]{1,0:T(8,128)(2,1)S(1)}, bf16[2048,128]{1,0:T(8,128)(2,1)S(1)}, u32[]{:S(2)}, u32[]{:S(2)}) collective-permute-start(bf16[2048,128]{1,0:T(8,128)(2,1)S(1)} %maximum_select_fusion.5), channel_id=1, source_target_pairs={{0,16},{4,20},{8,24},{12,28},{16,0},{20,4},{24,8},{28,12},{1,17},{... | collective-permute-start | bytes 1572872 | tf_op jit(solution)/shard_map/ppermute | solution.py:15
  342.7 52.4 %reduce-scatter.17.cloned.1.call-start = ((), (), s32[]{:S(2)}) async-start(), calls=%async_computation.15 | async-start | bytes 1310720 | tf_op jit(solution)/shard_map/reduce_scatter | solution.py:42
  361.6 33.6 %copy-start.1 = (f32[512,128]{1,0:T(8,128)S(1)}, f32[512,128]{1,0:T(8,128)}, u32[]{:S(2)}) copy-start(f32[512,128]{1,0:T(8,128)} %reduce-scatter.7.cloned.1.call-done) | copy-start | bytes 786436
  361.6 33.6 %copy-start.2 = (f32[512,128]{1,0:T(8,128)S(1)}, f32[512,128]{1,0:T(8,128)}, u32[]{:S(2)}) copy-start(f32[512,128]{1,0:T(8,128)} %reduce-scatter.13.cloned.1.call-done) | copy-start | bytes 786436
  361.6 33.6 %copy-start.3 = (f32[512,128]{1,0:T(8,128)S(1)}, f32[512,128]{1,0:T(8,128)}, u32[]{:S(2)}) copy-start(f32[512,128]{1,0:T(8,128)} %reduce-scatter.9.cloned.1.call-done) | copy-start | bytes 786436
  361.6 33.6 %copy-start.4 = (f32[512,128]{1,0:T(8,128)S(1)}, f32[512,128]{1,0:T(8,128)}, u32[]{:S(2)}) copy-start(f32[512,128]{1,0:T(8,128)} %reduce-scatter.15.cloned.1.call-done) | copy-start | bytes 786436
Sparse Core Ops, SparseCore 0:
  36.3 54.9 all-gather.3
  177.8 54.8 all-gather.5
  290.8 54.8 all-gather.7
Sparse Core Ops, SparseCore 1:
  117.4 24.3 reduce-scatter.6
  144.3 24.8 reduce-scatter.12
  229.8 24.8 reduce-scatter.8
  257.3 24.8 reduce-scatter.14
  342.8 24.7 reduce-scatter.10
  370.3 24.8 reduce-scatter.16
